TPU v7x, 512 devices: a whole 4x4x16 slice. The times are simulated.
512 devices in a mesh: leaf: 512 (over x, z, y, core).
Axes of the slice: x: 4, y: 4, z: 16, core: 2. Of those that a mesh axis runs over, the one named last changes fastest.
Arguments:
- rhs: float32 [262144, 512], P('leaf'), may hold values from -6 to 6
- leaf_inverse: float32 [262144, 512], P('leaf'), may hold values from -0.25 to 0.25
- basis: float32 [262144, 576], P('leaf'), may hold values from -0.25 to 0.25
- caps: float32 [512, 9, 128, 128], P('leaf'), as said below
Outputs:
- solution: float32 [262144, 512], P('leaf')
Inputs may be any that keep to these rules, and one draw needn't show every extreme that they name: caps[d, l] is equal for all leaves d with the same d // 2 ** (l + 1).
All inputs are finite; a program needn't handle non-finite values.
Results may differ from a plain program's by a relative error of at most 0.00014.
Values sent between devices are 32-bit elements; how exact they have to be, the bound alone decides.
No kernel may reach another device: no remote copies, remote signals or barrier semaphores. Data moves between devices by JAX's collectives and lax.ppermute only.
A program may use at most 64 MiB of HBM per device.

v0:
```python
import jax
import jax.numpy as jnp
from jax import lax
from jax.sharding import PartitionSpec as P

HIGH = lax.Precision.HIGHEST


def swapped(array, axis, apart):
    return lax.ppermute(array, axis, [(i, i ^ 1 << apart) for i in range(lax.axis_size(axis))])


def doubling_sum(local_term, level_index, half_bit):
    own_sum = local_term
    for bit_index in range(level_index):
        own_sum = own_sum + swapped(own_sum, "leaf", bit_index)
    other_sum = swapped(own_sum, "leaf", level_index)
    lower_half = jnp.where(half_bit == 0, own_sum, other_sum)
    upper_half = jnp.where(half_bit == 0, other_sum, own_sum)
    return jnp.concatenate([lower_half, upper_half], axis=0)


def local(rhs, leaf_inverse, basis, caps):
    iterate = jnp.dot(leaf_inverse, rhs, precision=HIGH, preferred_element_type=jnp.float32)
    device_count = lax.axis_size("leaf")
    level_count = device_count.bit_length() - 1
    rank_size = caps.shape[2] // 2
    position = lax.axis_index("leaf")
    for level_index in range(level_count):
        level_basis = basis[:, level_index * rank_size : (level_index + 1) * rank_size]
        local_term = lax.dot_general(
            level_basis,
            iterate,
            (((0,), (0,)), ((), ())),
            precision=HIGH,
            preferred_element_type=jnp.float32,
        )
        half_bit = position >> level_index & 1
        coupled = doubling_sum(local_term, level_index, half_bit)
        cap_rows = lax.dynamic_slice_in_dim(
            caps[0, level_index], half_bit * rank_size, rank_size, 0
        )
        correction = jnp.dot(cap_rows, coupled, precision=HIGH, preferred_element_type=jnp.float32)
        iterate = iterate - jnp.dot(
            level_basis, correction, precision=HIGH, preferred_element_type=jnp.float32
        )
    return iterate


def solution(mesh):
    return jax.shard_map(
        local,
        mesh=mesh,
        in_specs=(P("leaf", None), P("leaf", None), P("leaf", None), P("leaf", None, None, None)),
        out_specs=P("leaf", None),
        check_vma=False,
    )
```

profile of v0, /device:TPU:1, one launch (start us, length us, event | category | flops | bytes accessed | tf_op | source)
XLA Modules:
  0.0 420.7 jit_solution(8025081703921831728)
XLA Ops:
  1.2 3.1 fusion.100
  6.1 8.8 %collective-permute-start = (f32[64,512]{1,0:T(8,128)S(1)}, f32[64,512]{1,0:T(8,128)S(1)}, u32[]{:S(2)}, u32[]{:S(2)}) collective-permute-start(f32[64,512]{1,0:T(8,128)S(1)} %convolution_bitcast_fusion.17), channel_id=1, source_target_pairs={{0,1},{1,0},{2,3},{3,2},{4,5},{5,4},{6,7},{7,6},{8,9},{9,8},{10,11... | collective-permute-start | bytes 393224 | tf_op jit(solution)/shard_map/ppermute | solution.py:10
  19.8 2.3 collective-permute-start.1
  25.0 4.7 %collective-permute-done.2 = f32[64,512]{1,0:T(8,128)S(1)} collective-permute-done((f32[64,512]{1,0:T(8,128)S(1)}, f32[64,512]{1,0:T(8,128)S(1)}, u32[]{:S(2)}, u32[]{:S(2)}) %collective-permute-start.2) | collective-permute-done | bytes 131104 | tf_op jit(solution)/shard_map/ppermute | solution.py:10
  33.7 3.1 collective-permute-start.3
  39.7 4.7 %collective-permute-done.4 = f32[64,512]{1,0:T(8,128)S(1)} collective-permute-done((f32[64,512]{1,0:T(8,128)S(1)}, f32[64,512]{1,0:T(8,128)S(1)}, u32[]{:S(2)}, u32[]{:S(2)}) %collective-permute-start.4) | collective-permute-done | bytes 131104 | tf_op jit(solution)/shard_map/ppermute | solution.py:10
  46.3 5.3 %collective-permute-done.5 = f32[64,512]{1,0:T(8,128)S(1)} collective-permute-done((f32[64,512]{1,0:T(8,128)S(1)}, f32[64,512]{1,0:T(8,128)S(1)}, u32[]{:S(2)}, u32[]{:S(2)}) %collective-permute-start.5) | collective-permute-done | bytes 131104 | tf_op jit(solution)/shard_map/ppermute | solution.py:10
  51.9 1.9 fusion.6
  55.6 4.2 %collective-permute-start.6 = (f32[64,512]{1,0:T(8,128)S(1)}, f32[64,512]{1,0:T(8,128)S(1)}, u32[]{:S(2)}, u32[]{:S(2)}) collective-permute-start(f32[64,512]{1,0:T(8,128)S(1)} %convolution_bitcast_fusion.14), channel_id=1, source_target_pairs={{0,1},{1,0},{2,3},{3,2},{4,5},{5,4},{6,7},{7,6},{8,9},{9,8},{10,11... | collective-permute-start | bytes 393224 | tf_op jit(solution)/shard_map/ppermute | solution.py:10
  62.7 4.7 %collective-permute-done.7 = f32[64,512]{1,0:T(8,128)S(1)} collective-permute-done((f32[64,512]{1,0:T(8,128)S(1)}, f32[64,512]{1,0:T(8,128)S(1)}, u32[]{:S(2)}, u32[]{:S(2)}) %collective-permute-start.7) | collective-permute-done | bytes 131104 | tf_op jit(solution)/shard_map/ppermute | solution.py:10
  69.4 5.3 %collective-permute-done.8 = f32[64,512]{1,0:T(8,128)S(1)} collective-permute-done((f32[64,512]{1,0:T(8,128)S(1)}, f32[64,512]{1,0:T(8,128)S(1)}, u32[]{:S(2)}, u32[]{:S(2)}) %collective-permute-start.8) | collective-permute-done | bytes 131104 | tf_op jit(solution)/shard_map/ppermute | solution.py:10
  76.6 3.8 collective-permute-done.9
  84.3 5.4 %collective-permute-start.10 = (f32[64,512]{1,0:T(8,128)S(1)}, f32[64,512]{1,0:T(8,128)S(1)}, u32[]{:S(2)}, u32[]{:S(2)}) collective-permute-start(f32[64,512]{1,0:T(8,128)S(1)} %convolution_bitcast_fusion.13), channel_id=1, source_target_pairs={{0,1},{1,0},{2,3},{3,2},{4,5},{5,4},{6,7},{7,6},{8,9},{9,8},{10,11... | collective-permute-start | bytes 393224 | tf_op jit(solution)/shard_map/ppermute | solution.py:10
  92.7 4.7 %collective-permute-done.11 = f32[64,512]{1,0:T(8,128)S(1)} collective-permute-done((f32[64,512]{1,0:T(8,128)S(1)}, f32[64,512]{1,0:T(8,128)S(1)}, u32[]{:S(2)}, u32[]{:S(2)}) %collective-permute-start.11) | collective-permute-done | bytes 131104 | tf_op jit(solution)/shard_map/ppermute | solution.py:10
  99.3 5.3 %collective-permute-done.12 = f32[64,512]{1,0:T(8,128)S(1)} collective-permute-done((f32[64,512]{1,0:T(8,128)S(1)}, f32[64,512]{1,0:T(8,128)S(1)}, u32[]{:S(2)}, u32[]{:S(2)}) %collective-permute-start.12) | collective-permute-done | bytes 131104 | tf_op jit(solution)/shard_map/ppermute | solution.py:10
  106.5 3.8 collective-permute-done.13
  110.3 2.1 collective-permute-start.14
  112.5 5.6 %collective-permute-done.14 = f32[64,512]{1,0:T(8,128)S(1)} collective-permute-done((f32[64,512]{1,0:T(8,128)S(1)}, f32[64,512]{1,0:T(8,128)S(1)}, u32[]{:S(2)}, u32[]{:S(2)}) %collective-permute-start.14) | collective-permute-done | bytes 131104 | tf_op jit(solution)/shard_map/ppermute | solution.py:10
  122.0 6.3 %collective-permute-start.15 = (f32[64,512]{1,0:T(8,128)S(1)}, f32[64,512]{1,0:T(8,128)S(1)}, u32[]{:S(2)}, u32[]{:S(2)}) collective-permute-start(f32[64,512]{1,0:T(8,128)S(1)} %convolution_bitcast_fusion.12), channel_id=1, source_target_pairs={{0,1},{1,0},{2,3},{3,2},{4,5},{5,4},{6,7},{7,6},{8,9},{9,8},{10,11... | collective-permute-start | bytes 393224 | tf_op jit(solution)/shard_map/ppermute | solution.py:10
  131.2 4.7 %collective-permute-done.16 = f32[64,512]{1,0:T(8,128)S(1)} collective-permute-done((f32[64,512]{1,0:T(8,128)S(1)}, f32[64,512]{1,0:T(8,128)S(1)}, u32[]{:S(2)}, u32[]{:S(2)}) %collective-permute-start.16) | collective-permute-done | bytes 131104 | tf_op jit(solution)/shard_map/ppermute | solution.py:10
  137.8 5.3 %collective-permute-done.17 = f32[64,512]{1,0:T(8,128)S(1)} collective-permute-done((f32[64,512]{1,0:T(8,128)S(1)}, f32[64,512]{1,0:T(8,128)S(1)}, u32[]{:S(2)}, u32[]{:S(2)}) %collective-permute-start.17) | collective-permute-done | bytes 131104 | tf_op jit(solution)/shard_map/ppermute | solution.py:10
  145.1 3.8 collective-permute-done.18
  150.8 5.8 %collective-permute-done.19 = f32[64,512]{1,0:T(8,128)S(1)} collective-permute-done((f32[64,512]{1,0:T(8,128)S(1)}, f32[64,512]{1,0:T(8,128)S(1)}, u32[]{:S(2)}, u32[]{:S(2)}) %collective-permute-start.19) | collective-permute-done | bytes 131104 | tf_op jit(solution)/shard_map/ppermute | solution.py:10
  156.7 4.6 %collective-permute-start.20 = (f32[64,512]{1,0:T(8,128)S(1)}, f32[64,512]{1,0:T(8,128)S(1)}, u32[]{:S(2)}, u32[]{:S(2)}) collective-permute-start(f32[64,512]{1,0:T(8,128)S(1)} %add.155), channel_id=1, source_target_pairs={{0,32},{1,33},{2,34},{3,35},{4,36},{5,37},{6,38},{7,39},{8,40},{9,... | collective-permute-start | bytes 393224 | tf_op jit(solution)/shard_map/ppermute | solution.py:10
  161.3 13.1 %collective-permute-done.20 = f32[64,512]{1,0:T(8,128)S(1)} collective-permute-done((f32[64,512]{1,0:T(8,128)S(1)}, f32[64,512]{1,0:T(8,128)S(1)}, u32[]{:S(2)}, u32[]{:S(2)}) %collective-permute-start.20) | collective-permute-done | bytes 131104 | tf_op jit(solution)/shard_map/ppermute | solution.py:10
  178.4 3.0 collective-permute-start.21
  182.3 2.3 collective-permute-start.22
  184.7 4.3 %collective-permute-done.22 = f32[64,512]{1,0:T(8,128)S(1)} collective-permute-done((f32[64,512]{1,0:T(8,128)S(1)}, f32[64,512]{1,0:T(8,128)S(1)}, u32[]{:S(2)}, u32[]{:S(2)}) %collective-permute-start.22) | collective-permute-done | bytes 131104 | tf_op jit(solution)/shard_map/ppermute | solution.py:10
  189.0 3.5 collective-permute-start.23
  192.5 3.7 collective-permute-done.23
  198.1 3.8 collective-permute-done.24
  203.9 5.8 %collective-permute-done.25 = f32[64,512]{1,0:T(8,128)S(1)} collective-permute-done((f32[64,512]{1,0:T(8,128)S(1)}, f32[64,512]{1,0:T(8,128)S(1)}, u32[]{:S(2)}, u32[]{:S(2)}) %collective-permute-start.25) | collective-permute-done | bytes 131104 | tf_op jit(solution)/shard_map/ppermute | solution.py:10
  209.7 4.6 %collective-permute-start.26 = (f32[64,512]{1,0:T(8,128)S(1)}, f32[64,512]{1,0:T(8,128)S(1)}, u32[]{:S(2)}, u32[]{:S(2)}) collective-permute-start(f32[64,512]{1,0:T(8,128)S(1)} %add.161), channel_id=1, source_target_pairs={{0,32},{1,33},{2,34},{3,35},{4,36},{5,37},{6,38},{7,39},{8,40},{9,... | collective-permute-start | bytes 393224 | tf_op jit(solution)/shard_map/ppermute | solution.py:10
  214.4 13.1 %collective-permute-done.26 = f32[64,512]{1,0:T(8,128)S(1)} collective-permute-done((f32[64,512]{1,0:T(8,128)S(1)}, f32[64,512]{1,0:T(8,128)S(1)}, u32[]{:S(2)}, u32[]{:S(2)}) %collective-permute-start.26) | collective-permute-done | bytes 131104 | tf_op jit(solution)/shard_map/ppermute | solution.py:10
  227.5 11.3 %collective-permute-start.27 = (f32[64,512]{1,0:T(8,128)S(1)}, f32[64,512]{1,0:T(8,128)S(1)}, u32[]{:S(2)}, u32[]{:S(2)}) collective-permute-start(f32[64,512]{1,0:T(8,128)S(1)} %add.162), channel_id=1, source_target_pairs={{0,64},{1,65},{2,66},{3,67},{4,68},{5,69},{6,70},{7,71},{8,72},{9,... | collective-permute-start | bytes 393224 | tf_op jit(solution)/shard_map/ppermute | solution.py:10
  238.9 5.0 %collective-permute-done.27 = f32[64,512]{1,0:T(8,128)S(1)} collective-permute-done((f32[64,512]{1,0:T(8,128)S(1)}, f32[64,512]{1,0:T(8,128)S(1)}, u32[]{:S(2)}, u32[]{:S(2)}) %collective-permute-start.27) | collective-permute-done | bytes 131104 | tf_op jit(solution)/shard_map/ppermute | solution.py:10
  244.2 1.9 fusion.2
  247.8 8.1 %collective-permute-start.28 = (f32[64,512]{1,0:T(8,128)S(1)}, f32[64,512]{1,0:T(8,128)S(1)}, u32[]{:S(2)}, u32[]{:S(2)}) collective-permute-start(f32[64,512]{1,0:T(8,128)S(1)} %convolution_bitcast_fusion.10), channel_id=1, source_target_pairs={{0,1},{1,0},{2,3},{3,2},{4,5},{5,4},{6,7},{7,6},{8,9},{9,8},{10,11... | collective-permute-start | bytes 393224 | tf_op jit(solution)/shard_map/ppermute | solution.py:10
  256.9 3.2 collective-permute-start.29
  260.1 3.4 collective-permute-done.29
  263.6 5.3 %collective-permute-start.30 = (f32[64,512]{1,0:T(8,128)S(1)}, f32[64,512]{1,0:T(8,128)S(1)}, u32[]{:S(2)}, u32[]{:S(2)}) collective-permute-start(f32[64,512]{1,0:T(8,128)S(1)} %add.165), channel_id=1, source_target_pairs={{0,4},{1,5},{2,6},{3,7},{4,0},{5,1},{6,2},{7,3},{8,12},{9,13},{10,... | collective-permute-start | bytes 393224 | tf_op jit(solution)/shard_map/ppermute | solution.py:10
  268.9 2.3 collective-permute-done.30
  273.2 3.8 collective-permute-done.31
  278.9 5.8 %collective-permute-done.32 = f32[64,512]{1,0:T(8,128)S(1)} collective-permute-done((f32[64,512]{1,0:T(8,128)S(1)}, f32[64,512]{1,0:T(8,128)S(1)}, u32[]{:S(2)}, u32[]{:S(2)}) %collective-permute-start.32) | collective-permute-done | bytes 131104 | tf_op jit(solution)/shard_map/ppermute | solution.py:10
  284.7 4.3 %collective-permute-start.33 = (f32[64,512]{1,0:T(8,128)S(1)}, f32[64,512]{1,0:T(8,128)S(1)}, u32[]{:S(2)}, u32[]{:S(2)}) collective-permute-start(f32[64,512]{1,0:T(8,128)S(1)} %add.168), channel_id=1, source_target_pairs={{0,32},{1,33},{2,34},{3,35},{4,36},{5,37},{6,38},{7,39},{8,40},{9,... | collective-permute-start | bytes 393224 | tf_op jit(solution)/shard_map/ppermute | solution.py:10
  289.1 13.7 %collective-permute-done.33 = f32[64,512]{1,0:T(8,128)S(1)} collective-permute-done((f32[64,512]{1,0:T(8,128)S(1)}, f32[64,512]{1,0:T(8,128)S(1)}, u32[]{:S(2)}, u32[]{:S(2)}) %collective-permute-start.33) | collective-permute-done | bytes 131104 | tf_op jit(solution)/shard_map/ppermute | solution.py:10
  302.8 6.8 %collective-permute-start.34 = (f32[64,512]{1,0:T(8,128)S(1)}, f32[64,512]{1,0:T(8,128)S(1)}, u32[]{:S(2)}, u32[]{:S(2)}) collective-permute-start(f32[64,512]{1,0:T(8,128)S(1)} %add.169), channel_id=1, source_target_pairs={{0,64},{1,65},{2,66},{3,67},{4,68},{5,69},{6,70},{7,71},{8,72},{9,... | collective-permute-start | bytes 393224 | tf_op jit(solution)/shard_map/ppermute | solution.py:10
  309.6 13.6 %collective-permute-done.34 = f32[64,512]{1,0:T(8,128)S(1)} collective-permute-done((f32[64,512]{1,0:T(8,128)S(1)}, f32[64,512]{1,0:T(8,128)S(1)}, u32[]{:S(2)}, u32[]{:S(2)}) %collective-permute-start.34) | collective-permute-done | bytes 131104 | tf_op jit(solution)/shard_map/ppermute | solution.py:10
  325.2 4.5 %collective-permute-done.35 = f32[64,512]{1,0:T(8,128)S(1)} collective-permute-done((f32[64,512]{1,0:T(8,128)S(1)}, f32[64,512]{1,0:T(8,128)S(1)}, u32[]{:S(2)}, u32[]{:S(2)}) %collective-permute-start.35) | collective-permute-done | bytes 131104 | tf_op jit(solution)/shard_map/ppermute | solution.py:10
  333.7 3.2 collective-permute-start.36
  339.8 4.7 %collective-permute-done.37 = f32[64,512]{1,0:T(8,128)S(1)} collective-permute-done((f32[64,512]{1,0:T(8,128)S(1)}, f32[64,512]{1,0:T(8,128)S(1)}, u32[]{:S(2)}, u32[]{:S(2)}) %collective-permute-start.37) | collective-permute-done | bytes 131104 | tf_op jit(solution)/shard_map/ppermute | solution.py:10
  344.6 3.6 collective-permute-start.38
  348.2 3.6 collective-permute-done.38
  353.7 3.8 collective-permute-done.39
  359.5 5.8 %collective-permute-done.40 = f32[64,512]{1,0:T(8,128)S(1)} collective-permute-done((f32[64,512]{1,0:T(8,128)S(1)}, f32[64,512]{1,0:T(8,128)S(1)}, u32[]{:S(2)}, u32[]{:S(2)}) %collective-permute-start.40) | collective-permute-done | bytes 131104 | tf_op jit(solution)/shard_map/ppermute | solution.py:10
  365.3 4.4 %collective-permute-start.41 = (f32[64,512]{1,0:T(8,128)S(1)}, f32[64,512]{1,0:T(8,128)S(1)}, u32[]{:S(2)}, u32[]{:S(2)}) collective-permute-start(f32[64,512]{1,0:T(8,128)S(1)} %add.176), channel_id=1, source_target_pairs={{0,32},{1,33},{2,34},{3,35},{4,36},{5,37},{6,38},{7,39},{8,40},{9,... | collective-permute-start | bytes 393224 | tf_op jit(solution)/shard_map/ppermute | solution.py:10
  369.7 13.4 %collective-permute-done.41 = f32[64,512]{1,0:T(8,128)S(1)} collective-permute-done((f32[64,512]{1,0:T(8,128)S(1)}, f32[64,512]{1,0:T(8,128)S(1)}, u32[]{:S(2)}, u32[]{:S(2)}) %collective-permute-start.41) | collective-permute-done | bytes 131104 | tf_op jit(solution)/shard_map/ppermute | solution.py:10
  383.1 7.2 %collective-permute-start.42 = (f32[64,512]{1,0:T(8,128)S(1)}, f32[64,512]{1,0:T(8,128)S(1)}, u32[]{:S(2)}, u32[]{:S(2)}) collective-permute-start(f32[64,512]{1,0:T(8,128)S(1)} %add.177), channel_id=1, source_target_pairs={{0,64},{1,65},{2,66},{3,67},{4,68},{5,69},{6,70},{7,71},{8,72},{9,... | collective-permute-start | bytes 393224 | tf_op jit(solution)/shard_map/ppermute | solution.py:10
  390.2 13.6 %collective-permute-done.42 = f32[64,512]{1,0:T(8,128)S(1)} collective-permute-done((f32[64,512]{1,0:T(8,128)S(1)}, f32[64,512]{1,0:T(8,128)S(1)}, u32[]{:S(2)}, u32[]{:S(2)}) %collective-permute-start.42) | collective-permute-done | bytes 131104 | tf_op jit(solution)/shard_map/ppermute | solution.py:10
  403.9 2.0 collective-permute-start.43
  405.8 4.4 %collective-permute-done.43 = f32[64,512]{1,0:T(8,128)S(1)} collective-permute-done((f32[64,512]{1,0:T(8,128)S(1)}, f32[64,512]{1,0:T(8,128)S(1)}, u32[]{:S(2)}, u32[]{:S(2)}) %collective-permute-start.43) | collective-permute-done | bytes 131104 | tf_op jit(solution)/shard_map/ppermute | solution.py:10
  410.3 3.5 collective-permute-start.44
  413.9 3.7 collective-permute-done.44
  417.8 2.9 fusion
  (108 shorter events, 80.5 us)
Async XLA Ops:
  0.0 1.2 copy-start
  4.3 10.6 %copy-start.1 = (f32[1,9,128,128]{3,2,1,0:T(8,128)S(1)}, f32[1,9,128,128]{3,2,1,0:T(8,128)}, u32[]{:S(2)}) copy-start(f32[1,9,128,128]{3,2,1,0:T(8,128)} %param.7) | copy-start | bytes 1769476
  6.1 9.8 %collective-permute-start = (f32[64,512]{1,0:T(8,128)S(1)}, f32[64,512]{1,0:T(8,128)S(1)}, u32[]{:S(2)}, u32[]{:S(2)}) collective-permute-start(f32[64,512]{1,0:T(8,128)S(1)} %convolution_bitcast_fusion.17), channel_id=1, source_target_pairs={{0,1},{1,0},{2,3},{3,2},{4,5},{5,4},{6,7},{7,6},{8,9},{9,8},{10,11... | collective-permute-start | bytes 393224 | tf_op jit(solution)/shard_map/ppermute | solution.py:10
  18.1 11.6 %copy-start.3 = (f32[1,1,128,128]{3,2,1,0:T(8,128)S(1)}, f32[1,1,128,128]{3,2,1,0:T(8,128)}, u32[]{:S(2)}) copy-start(f32[1,1,128,128]{3,2,1,0:T(8,128)} %get-tuple-element.11) | copy-start | bytes 196612
  19.8 3.2 collective-permute-start.1
  23.1 6.6 %collective-permute-start.2 = (f32[64,512]{1,0:T(8,128)S(1)}, f32[64,512]{1,0:T(8,128)S(1)}, u32[]{:S(2)}, u32[]{:S(2)}) collective-permute-start(f32[64,512]{1,0:T(8,128)S(1)} %add.137), channel_id=1, source_target_pairs={{0,2},{1,3},{2,0},{3,1},{4,6},{5,7},{6,4},{7,5},{8,10},{9,11},{10,... | collective-permute-start | bytes 393224 | tf_op jit(solution)/shard_map/ppermute | solution.py:10
  31.9 19.7 %copy-start.2 = (f32[1,1,128,128]{3,2,1,0:T(8,128)S(1)}, f32[1,1,128,128]{3,2,1,0:T(8,128)}, u32[]{:S(2)}) copy-start(f32[1,1,128,128]{3,2,1,0:T(8,128)} %get-tuple-element.10) | copy-start | bytes 196612
  33.7 4.1 collective-permute-start.3
  37.8 6.6 %collective-permute-start.4 = (f32[64,512]{1,0:T(8,128)S(1)}, f32[64,512]{1,0:T(8,128)S(1)}, u32[]{:S(2)}, u32[]{:S(2)}) collective-permute-start(f32[64,512]{1,0:T(8,128)S(1)} %add.139), channel_id=1, source_target_pairs={{0,2},{1,3},{2,0},{3,1},{4,6},{5,7},{6,4},{7,5},{8,10},{9,11},{10,... | collective-permute-start | bytes 393224 | tf_op jit(solution)/shard_map/ppermute | solution.py:10
  44.4 7.2 %collective-permute-start.5 = (f32[64,512]{1,0:T(8,128)S(1)}, f32[64,512]{1,0:T(8,128)S(1)}, u32[]{:S(2)}, u32[]{:S(2)}) collective-permute-start(f32[64,512]{1,0:T(8,128)S(1)} %add.140), channel_id=1, source_target_pairs={{0,4},{1,5},{2,6},{3,7},{4,0},{5,1},{6,2},{7,3},{8,12},{9,13},{10,... | collective-permute-start | bytes 393224 | tf_op jit(solution)/shard_map/ppermute | solution.py:10
  55.6 5.2 %collective-permute-start.6 = (f32[64,512]{1,0:T(8,128)S(1)}, f32[64,512]{1,0:T(8,128)S(1)}, u32[]{:S(2)}, u32[]{:S(2)}) collective-permute-start(f32[64,512]{1,0:T(8,128)S(1)} %convolution_bitcast_fusion.14), channel_id=1, source_target_pairs={{0,1},{1,0},{2,3},{3,2},{4,5},{5,4},{6,7},{7,6},{8,9},{9,8},{10,11... | collective-permute-start | bytes 393224 | tf_op jit(solution)/shard_map/ppermute | solution.py:10
  60.8 6.6 %collective-permute-start.7 = (f32[64,512]{1,0:T(8,128)S(1)}, f32[64,512]{1,0:T(8,128)S(1)}, u32[]{:S(2)}, u32[]{:S(2)}) collective-permute-start(f32[64,512]{1,0:T(8,128)S(1)} %add.142), channel_id=1, source_target_pairs={{0,2},{1,3},{2,0},{3,1},{4,6},{5,7},{6,4},{7,5},{8,10},{9,11},{10,... | collective-permute-start | bytes 393224 | tf_op jit(solution)/shard_map/ppermute | solution.py:10
  67.4 7.2 %collective-permute-start.8 = (f32[64,512]{1,0:T(8,128)S(1)}, f32[64,512]{1,0:T(8,128)S(1)}, u32[]{:S(2)}, u32[]{:S(2)}) collective-permute-start(f32[64,512]{1,0:T(8,128)S(1)} %add.143), channel_id=1, source_target_pairs={{0,4},{1,5},{2,6},{3,7},{4,0},{5,1},{6,2},{7,3},{8,12},{9,13},{10,... | collective-permute-start | bytes 393224 | tf_op jit(solution)/shard_map/ppermute | solution.py:10
  74.7 5.7 %collective-permute-start.9 = (f32[64,512]{1,0:T(8,128)S(1)}, f32[64,512]{1,0:T(8,128)S(1)}, u32[]{:S(2)}, u32[]{:S(2)}) collective-permute-start(f32[64,512]{1,0:T(8,128)S(1)} %add.144), channel_id=1, source_target_pairs={{0,8},{1,9},{2,10},{3,11},{4,12},{5,13},{6,14},{7,15},{8,0},{9,1},... | collective-permute-start | bytes 393224 | tf_op jit(solution)/shard_map/ppermute | solution.py:10
  84.3 6.4 %collective-permute-start.10 = (f32[64,512]{1,0:T(8,128)S(1)}, f32[64,512]{1,0:T(8,128)S(1)}, u32[]{:S(2)}, u32[]{:S(2)}) collective-permute-start(f32[64,512]{1,0:T(8,128)S(1)} %convolution_bitcast_fusion.13), channel_id=1, source_target_pairs={{0,1},{1,0},{2,3},{3,2},{4,5},{5,4},{6,7},{7,6},{8,9},{9,8},{10,11... | collective-permute-start | bytes 393224 | tf_op jit(solution)/shard_map/ppermute | solution.py:10
  90.7 6.6 %collective-permute-start.11 = (f32[64,512]{1,0:T(8,128)S(1)}, f32[64,512]{1,0:T(8,128)S(1)}, u32[]{:S(2)}, u32[]{:S(2)}) collective-permute-start(f32[64,512]{1,0:T(8,128)S(1)} %add.146), channel_id=1, source_target_pairs={{0,2},{1,3},{2,0},{3,1},{4,6},{5,7},{6,4},{7,5},{8,10},{9,11},{10,... | collective-permute-start | bytes 393224 | tf_op jit(solution)/shard_map/ppermute | solution.py:10
  97.4 7.2 %collective-permute-start.12 = (f32[64,512]{1,0:T(8,128)S(1)}, f32[64,512]{1,0:T(8,128)S(1)}, u32[]{:S(2)}, u32[]{:S(2)}) collective-permute-start(f32[64,512]{1,0:T(8,128)S(1)} %add.147), channel_id=1, source_target_pairs={{0,4},{1,5},{2,6},{3,7},{4,0},{5,1},{6,2},{7,3},{8,12},{9,13},{10,... | collective-permute-start | bytes 393224 | tf_op jit(solution)/shard_map/ppermute | solution.py:10
  104.6 5.7 %collective-permute-start.13 = (f32[64,512]{1,0:T(8,128)S(1)}, f32[64,512]{1,0:T(8,128)S(1)}, u32[]{:S(2)}, u32[]{:S(2)}) collective-permute-start(f32[64,512]{1,0:T(8,128)S(1)} %add.148), channel_id=1, source_target_pairs={{0,8},{1,9},{2,10},{3,11},{4,12},{5,13},{6,14},{7,15},{8,0},{9,1},... | collective-permute-start | bytes 393224 | tf_op jit(solution)/shard_map/ppermute | solution.py:10
  110.3 7.7 %collective-permute-start.14 = (f32[64,512]{1,0:T(8,128)S(1)}, f32[64,512]{1,0:T(8,128)S(1)}, u32[]{:S(2)}, u32[]{:S(2)}) collective-permute-start(f32[64,512]{1,0:T(8,128)S(1)} %add.149), channel_id=1, source_target_pairs={{0,16},{1,17},{2,18},{3,19},{4,20},{5,21},{6,22},{7,23},{8,24},{9,... | collective-permute-start | bytes 393224 | tf_op jit(solution)/shard_map/ppermute | solution.py:10
  122.0 7.2 %collective-permute-start.15 = (f32[64,512]{1,0:T(8,128)S(1)}, f32[64,512]{1,0:T(8,128)S(1)}, u32[]{:S(2)}, u32[]{:S(2)}) collective-permute-start(f32[64,512]{1,0:T(8,128)S(1)} %convolution_bitcast_fusion.12), channel_id=1, source_target_pairs={{0,1},{1,0},{2,3},{3,2},{4,5},{5,4},{6,7},{7,6},{8,9},{9,8},{10,11... | collective-permute-start | bytes 393224 | tf_op jit(solution)/shard_map/ppermute | solution.py:10
  129.3 6.6 %collective-permute-start.16 = (f32[64,512]{1,0:T(8,128)S(1)}, f32[64,512]{1,0:T(8,128)S(1)}, u32[]{:S(2)}, u32[]{:S(2)}) collective-permute-start(f32[64,512]{1,0:T(8,128)S(1)} %add.151), channel_id=1, source_target_pairs={{0,2},{1,3},{2,0},{3,1},{4,6},{5,7},{6,4},{7,5},{8,10},{9,11},{10,... | collective-permute-start | bytes 393224 | tf_op jit(solution)/shard_map/ppermute | solution.py:10
  135.9 7.2 %collective-permute-start.17 = (f32[64,512]{1,0:T(8,128)S(1)}, f32[64,512]{1,0:T(8,128)S(1)}, u32[]{:S(2)}, u32[]{:S(2)}) collective-permute-start(f32[64,512]{1,0:T(8,128)S(1)} %add.152), channel_id=1, source_target_pairs={{0,4},{1,5},{2,6},{3,7},{4,0},{5,1},{6,2},{7,3},{8,12},{9,13},{10,... | collective-permute-start | bytes 393224 | tf_op jit(solution)/shard_map/ppermute | solution.py:10
  143.2 5.7 %collective-permute-start.18 = (f32[64,512]{1,0:T(8,128)S(1)}, f32[64,512]{1,0:T(8,128)S(1)}, u32[]{:S(2)}, u32[]{:S(2)}) collective-permute-start(f32[64,512]{1,0:T(8,128)S(1)} %add.153), channel_id=1, source_target_pairs={{0,8},{1,9},{2,10},{3,11},{4,12},{5,13},{6,14},{7,15},{8,0},{9,1},... | collective-permute-start | bytes 393224 | tf_op jit(solution)/shard_map/ppermute | solution.py:10
  148.9 7.7 %collective-permute-start.19 = (f32[64,512]{1,0:T(8,128)S(1)}, f32[64,512]{1,0:T(8,128)S(1)}, u32[]{:S(2)}, u32[]{:S(2)}) collective-permute-start(f32[64,512]{1,0:T(8,128)S(1)} %add.154), channel_id=1, source_target_pairs={{0,16},{1,17},{2,18},{3,19},{4,20},{5,21},{6,22},{7,23},{8,24},{9,... | collective-permute-start | bytes 393224 | tf_op jit(solution)/shard_map/ppermute | solution.py:10
  156.7 17.8 %collective-permute-start.20 = (f32[64,512]{1,0:T(8,128)S(1)}, f32[64,512]{1,0:T(8,128)S(1)}, u32[]{:S(2)}, u32[]{:S(2)}) collective-permute-start(f32[64,512]{1,0:T(8,128)S(1)} %add.155), channel_id=1, source_target_pairs={{0,32},{1,33},{2,34},{3,35},{4,36},{5,37},{6,38},{7,39},{8,40},{9,... | collective-permute-start | bytes 393224 | tf_op jit(solution)/shard_map/ppermute | solution.py:10
  178.4 3.9 collective-permute-start.21
  182.3 6.6 %collective-permute-start.22 = (f32[64,512]{1,0:T(8,128)S(1)}, f32[64,512]{1,0:T(8,128)S(1)}, u32[]{:S(2)}, u32[]{:S(2)}) collective-permute-start(f32[64,512]{1,0:T(8,128)S(1)} %add.157), channel_id=1, source_target_pairs={{0,2},{1,3},{2,0},{3,1},{4,6},{5,7},{6,4},{7,5},{8,10},{9,11},{10,... | collective-permute-start | bytes 393224 | tf_op jit(solution)/shard_map/ppermute | solution.py:10
  189.0 7.2 %collective-permute-start.23 = (f32[64,512]{1,0:T(8,128)S(1)}, f32[64,512]{1,0:T(8,128)S(1)}, u32[]{:S(2)}, u32[]{:S(2)}) collective-permute-start(f32[64,512]{1,0:T(8,128)S(1)} %add.158), channel_id=1, source_target_pairs={{0,4},{1,5},{2,6},{3,7},{4,0},{5,1},{6,2},{7,3},{8,12},{9,13},{10,... | collective-permute-start | bytes 393224 | tf_op jit(solution)/shard_map/ppermute | solution.py:10
  196.2 5.7 %collective-permute-start.24 = (f32[64,512]{1,0:T(8,128)S(1)}, f32[64,512]{1,0:T(8,128)S(1)}, u32[]{:S(2)}, u32[]{:S(2)}) collective-permute-start(f32[64,512]{1,0:T(8,128)S(1)} %add.159), channel_id=1, source_target_pairs={{0,8},{1,9},{2,10},{3,11},{4,12},{5,13},{6,14},{7,15},{8,0},{9,1},... | collective-permute-start | bytes 393224 | tf_op jit(solution)/shard_map/ppermute | solution.py:10
  201.9 7.7 %collective-permute-start.25 = (f32[64,512]{1,0:T(8,128)S(1)}, f32[64,512]{1,0:T(8,128)S(1)}, u32[]{:S(2)}, u32[]{:S(2)}) collective-permute-start(f32[64,512]{1,0:T(8,128)S(1)} %add.160), channel_id=1, source_target_pairs={{0,16},{1,17},{2,18},{3,19},{4,20},{5,21},{6,22},{7,23},{8,24},{9,... | collective-permute-start | bytes 393224 | tf_op jit(solution)/shard_map/ppermute | solution.py:10
  209.7 17.8 %collective-permute-start.26 = (f32[64,512]{1,0:T(8,128)S(1)}, f32[64,512]{1,0:T(8,128)S(1)}, u32[]{:S(2)}, u32[]{:S(2)}) collective-permute-start(f32[64,512]{1,0:T(8,128)S(1)} %add.161), channel_id=1, source_target_pairs={{0,32},{1,33},{2,34},{3,35},{4,36},{5,37},{6,38},{7,39},{8,40},{9,... | collective-permute-start | bytes 393224 | tf_op jit(solution)/shard_map/ppermute | solution.py:10
  227.5 16.4 %collective-permute-start.27 = (f32[64,512]{1,0:T(8,128)S(1)}, f32[64,512]{1,0:T(8,128)S(1)}, u32[]{:S(2)}, u32[]{:S(2)}) collective-permute-start(f32[64,512]{1,0:T(8,128)S(1)} %add.162), channel_id=1, source_target_pairs={{0,64},{1,65},{2,66},{3,67},{4,68},{5,69},{6,70},{7,71},{8,72},{9,... | collective-permute-start | bytes 393224 | tf_op jit(solution)/shard_map/ppermute | solution.py:10
  247.8 9.1 %collective-permute-start.28 = (f32[64,512]{1,0:T(8,128)S(1)}, f32[64,512]{1,0:T(8,128)S(1)}, u32[]{:S(2)}, u32[]{:S(2)}) collective-permute-start(f32[64,512]{1,0:T(8,128)S(1)} %convolution_bitcast_fusion.10), channel_id=1, source_target_pairs={{0,1},{1,0},{2,3},{3,2},{4,5},{5,4},{6,7},{7,6},{8,9},{9,8},{10,11... | collective-permute-start | bytes 393224 | tf_op jit(solution)/shard_map/ppermute | solution.py:10
  256.9 6.6 %collective-permute-start.29 = (f32[64,512]{1,0:T(8,128)S(1)}, f32[64,512]{1,0:T(8,128)S(1)}, u32[]{:S(2)}, u32[]{:S(2)}) collective-permute-start(f32[64,512]{1,0:T(8,128)S(1)} %add.164), channel_id=1, source_target_pairs={{0,2},{1,3},{2,0},{3,1},{4,6},{5,7},{6,4},{7,5},{8,10},{9,11},{10,... | collective-permute-start | bytes 393224 | tf_op jit(solution)/shard_map/ppermute | solution.py:10
  263.6 7.7 %collective-permute-start.30 = (f32[64,512]{1,0:T(8,128)S(1)}, f32[64,512]{1,0:T(8,128)S(1)}, u32[]{:S(2)}, u32[]{:S(2)}) collective-permute-start(f32[64,512]{1,0:T(8,128)S(1)} %add.165), channel_id=1, source_target_pairs={{0,4},{1,5},{2,6},{3,7},{4,0},{5,1},{6,2},{7,3},{8,12},{9,13},{10,... | collective-permute-start | bytes 393224 | tf_op jit(solution)/shard_map/ppermute | solution.py:10
  271.2 5.7 %collective-permute-start.31 = (f32[64,512]{1,0:T(8,128)S(1)}, f32[64,512]{1,0:T(8,128)S(1)}, u32[]{:S(2)}, u32[]{:S(2)}) collective-permute-start(f32[64,512]{1,0:T(8,128)S(1)} %add.166), channel_id=1, source_target_pairs={{0,8},{1,9},{2,10},{3,11},{4,12},{5,13},{6,14},{7,15},{8,0},{9,1},... | collective-permute-start | bytes 393224 | tf_op jit(solution)/shard_map/ppermute | solution.py:10
  277.0 7.7 %collective-permute-start.32 = (f32[64,512]{1,0:T(8,128)S(1)}, f32[64,512]{1,0:T(8,128)S(1)}, u32[]{:S(2)}, u32[]{:S(2)}) collective-permute-start(f32[64,512]{1,0:T(8,128)S(1)} %add.167), channel_id=1, source_target_pairs={{0,16},{1,17},{2,18},{3,19},{4,20},{5,21},{6,22},{7,23},{8,24},{9,... | collective-permute-start | bytes 393224 | tf_op jit(solution)/shard_map/ppermute | solution.py:10
  284.7 18.0 %collective-permute-start.33 = (f32[64,512]{1,0:T(8,128)S(1)}, f32[64,512]{1,0:T(8,128)S(1)}, u32[]{:S(2)}, u32[]{:S(2)}) collective-permute-start(f32[64,512]{1,0:T(8,128)S(1)} %add.168), channel_id=1, source_target_pairs={{0,32},{1,33},{2,34},{3,35},{4,36},{5,37},{6,38},{7,39},{8,40},{9,... | collective-permute-start | bytes 393224 | tf_op jit(solution)/shard_map/ppermute | solution.py:10
  302.8 20.5 %collective-permute-start.34 = (f32[64,512]{1,0:T(8,128)S(1)}, f32[64,512]{1,0:T(8,128)S(1)}, u32[]{:S(2)}, u32[]{:S(2)}) collective-permute-start(f32[64,512]{1,0:T(8,128)S(1)} %add.169), channel_id=1, source_target_pairs={{0,64},{1,65},{2,66},{3,67},{4,68},{5,69},{6,70},{7,71},{8,72},{9,... | collective-permute-start | bytes 393224 | tf_op jit(solution)/shard_map/ppermute | solution.py:10
  323.3 6.5 %collective-permute-start.35 = (f32[64,512]{1,0:T(8,128)S(1)}, f32[64,512]{1,0:T(8,128)S(1)}, u32[]{:S(2)}, u32[]{:S(2)}) collective-permute-start(f32[64,512]{1,0:T(8,128)S(1)} %add.170), channel_id=1, source_target_pairs={{0,128},{1,129},{2,130},{3,131},{4,132},{5,133},{6,134},{7,135},{8... | collective-permute-start | bytes 393224 | tf_op jit(solution)/shard_map/ppermute | solution.py:10
  333.7 4.2 %collective-permute-start.36 = (f32[64,512]{1,0:T(8,128)S(1)}, f32[64,512]{1,0:T(8,128)S(1)}, u32[]{:S(2)}, u32[]{:S(2)}) collective-permute-start(f32[64,512]{1,0:T(8,128)S(1)} %convolution_bitcast_fusion.9), channel_id=1, source_target_pairs={{0,1},{1,0},{2,3},{3,2},{4,5},{5,4},{6,7},{7,6},{8,9},{9,8},{10,11... | collective-permute-start | bytes 393224 | tf_op jit(solution)/shard_map/ppermute | solution.py:10
  337.9 6.6 %collective-permute-start.37 = (f32[64,512]{1,0:T(8,128)S(1)}, f32[64,512]{1,0:T(8,128)S(1)}, u32[]{:S(2)}, u32[]{:S(2)}) collective-permute-start(f32[64,512]{1,0:T(8,128)S(1)} %add.172), channel_id=1, source_target_pairs={{0,2},{1,3},{2,0},{3,1},{4,6},{5,7},{6,4},{7,5},{8,10},{9,11},{10,... | collective-permute-start | bytes 393224 | tf_op jit(solution)/shard_map/ppermute | solution.py:10
  344.6 7.2 %collective-permute-start.38 = (f32[64,512]{1,0:T(8,128)S(1)}, f32[64,512]{1,0:T(8,128)S(1)}, u32[]{:S(2)}, u32[]{:S(2)}) collective-permute-start(f32[64,512]{1,0:T(8,128)S(1)} %add.173), channel_id=1, source_target_pairs={{0,4},{1,5},{2,6},{3,7},{4,0},{5,1},{6,2},{7,3},{8,12},{9,13},{10,... | collective-permute-start | bytes 393224 | tf_op jit(solution)/shard_map/ppermute | solution.py:10
  351.8 5.7 %collective-permute-start.39 = (f32[64,512]{1,0:T(8,128)S(1)}, f32[64,512]{1,0:T(8,128)S(1)}, u32[]{:S(2)}, u32[]{:S(2)}) collective-permute-start(f32[64,512]{1,0:T(8,128)S(1)} %add.174), channel_id=1, source_target_pairs={{0,8},{1,9},{2,10},{3,11},{4,12},{5,13},{6,14},{7,15},{8,0},{9,1},... | collective-permute-start | bytes 393224 | tf_op jit(solution)/shard_map/ppermute | solution.py:10
  357.5 7.7 %collective-permute-start.40 = (f32[64,512]{1,0:T(8,128)S(1)}, f32[64,512]{1,0:T(8,128)S(1)}, u32[]{:S(2)}, u32[]{:S(2)}) collective-permute-start(f32[64,512]{1,0:T(8,128)S(1)} %add.175), channel_id=1, source_target_pairs={{0,16},{1,17},{2,18},{3,19},{4,20},{5,21},{6,22},{7,23},{8,24},{9,... | collective-permute-start | bytes 393224 | tf_op jit(solution)/shard_map/ppermute | solution.py:10
  365.3 17.8 %collective-permute-start.41 = (f32[64,512]{1,0:T(8,128)S(1)}, f32[64,512]{1,0:T(8,128)S(1)}, u32[]{:S(2)}, u32[]{:S(2)}) collective-permute-start(f32[64,512]{1,0:T(8,128)S(1)} %add.176), channel_id=1, source_target_pairs={{0,32},{1,33},{2,34},{3,35},{4,36},{5,37},{6,38},{7,39},{8,40},{9,... | collective-permute-start | bytes 393224 | tf_op jit(solution)/shard_map/ppermute | solution.py:10
  383.1 20.7 %collective-permute-start.42 = (f32[64,512]{1,0:T(8,128)S(1)}, f32[64,512]{1,0:T(8,128)S(1)}, u32[]{:S(2)}, u32[]{:S(2)}) collective-permute-start(f32[64,512]{1,0:T(8,128)S(1)} %add.177), channel_id=1, source_target_pairs={{0,64},{1,65},{2,66},{3,67},{4,68},{5,69},{6,70},{7,71},{8,72},{9,... | collective-permute-start | bytes 393224 | tf_op jit(solution)/shard_map/ppermute | solution.py:10
  403.9 6.4 %collective-permute-start.43 = (f32[64,512]{1,0:T(8,128)S(1)}, f32[64,512]{1,0:T(8,128)S(1)}, u32[]{:S(2)}, u32[]{:S(2)}) collective-permute-start(f32[64,512]{1,0:T(8,128)S(1)} %add.178), channel_id=1, source_target_pairs={{0,128},{1,129},{2,130},{3,131},{4,132},{5,133},{6,134},{7,135},{8... | collective-permute-start | bytes 393224 | tf_op jit(solution)/shard_map/ppermute | solution.py:10
  410.3 7.2 %collective-permute-start.44 = (f32[64,512]{1,0:T(8,128)S(1)}, f32[64,512]{1,0:T(8,128)S(1)}, u32[]{:S(2)}, u32[]{:S(2)}) collective-permute-start(f32[64,512]{1,0:T(8,128)S(1)} %add.179), channel_id=1, source_target_pairs={{0,256},{1,257},{2,258},{3,259},{4,260},{5,261},{6,262},{7,263},{8... | collective-permute-start | bytes 393224 | tf_op jit(solution)/shard_map/ppermute | solution.py:10
where the time goes:
time: 422 us; the launch traced here: 421 us
  waiting for transfers between devices  224 us (53%)
  starting transfers between devices  154 us (36%)
  matrix products  39.2 us (9%)
    ppermute x45, waiting for transfers between devices, swapped(): lax.ppermute(array, axis, [(i, i ^ 1 << apart) for i in range(lax.axis_si...  224 us
    ppermute x45, starting transfers between devices, swapped(): lax.ppermute(array, axis, [(i, i ^ 1 << apart) for i in range(lax.axis_si...  154 us
    dot_general x9, matrix products, local(): jnp.dot(level_basis, correction, precision=HIGH, preferred_element_type=j...  18.4 us
    dot_general x9, matrix products, local(): lax.dot_general(level_basis, iterate, (((0,), (0,)), ((), ())), precision...  15.4 us
  transfers between devices with their start and end apart: 45, of which 45 were waited for; matrix products, arithmetic and copies ran while one was open for 0% of the time, Pallas kernels for 0%

commit v1 on v0

v1 whole, which is shorter than its diff:
```python
import jax
import jax.numpy as jnp
from jax import lax
from jax.sharding import PartitionSpec as P

HIGH = lax.Precision.HIGH
HIGHEST = lax.Precision.HIGHEST

RANK = 64
LEVELS = 9
PARTNER = (1, 2, 6, 8, 16, 32, 96, 128, 384)


def aligned(size, count):
    return [list(range(start, start + size)) for start in range(0, count, size)]


def dot(a, b, dims, precision):
    return lax.dot_general(a, b, ((dims[0], dims[1]), ((), ())), precision=precision,
                           preferred_element_type=jnp.float32)


def sent(array, mask):
    count = lax.axis_size("leaf")
    return lax.ppermute(array, "leaf", [(i, i ^ mask) for i in range(count)])


def step(own, other, gram_own, gram_other, cap):
    keep = own.shape[1] - RANK
    pair = jnp.concatenate([own[:, keep:], other[:, keep:]], axis=1)
    both = dot(pair, cap, ((1,), (1,)), HIGHEST)
    if keep == 0:
        return both, None
    gram = jnp.concatenate([gram_own, gram_other], axis=0)
    rest = own[:, :keep] + other[:, :keep] - dot(both, gram, ((1,), (0,)), HIGHEST)
    return both, rest


def local(rhs, leaf_inverse, basis, caps):
    count = lax.axis_size("leaf")
    position = lax.axis_index("leaf")
    bit = [position >> n & 1 for n in range(LEVELS)]
    core, y_low, y_high = bit[0], bit[1], bit[2]
    z_quarter = position >> 5 & 3
    z_half = position >> 6 & 1

    factors = basis.T
    factors = jnp.concatenate(
        [factors[l * RANK : (l + 1) * RANK] for l in range(LEVELS - 1, -1, -1)], axis=0
    )
    gram = dot(factors, factors, ((1,), (1,)), HIGH)

    def gram_row(level):
        top = (LEVELS - 1 - level) * RANK
        return gram[top : top + RANK, :top]

    row2 = gram_row(2)
    octet_part = jnp.concatenate(
        [jnp.where(y_high == 0, row2, 0.0), jnp.where(y_high == 1, row2, 0.0), gram[256:384, :384]],
        axis=0,
    )
    octet_sum = lax.psum(octet_part, "leaf", axis_index_groups=aligned(8, count))
    row5, row6, row7 = gram_row(5), gram_row(6), gram_row(7)
    slots5 = jnp.concatenate([jnp.where(z_quarter == s, row5, 0.0) for s in range(4)], axis=0)
    side7 = jnp.concatenate([row7, jnp.zeros((3 * RANK, RANK), jnp.float32)], axis=0)
    slots6 = jnp.concatenate([jnp.where(z_half == s, row6, 0.0) for s in range(2)], axis=1)
    plane_part = jnp.concatenate([jnp.concatenate([slots5, side7], axis=1), slots6], axis=0)
    plane_sum = lax.psum(plane_part, "leaf", axis_index_groups=aligned(128, count))

    turned = jnp.roll(caps[0], (RANK, RANK), (1, 2))
    half_bits = jnp.stack(bit)[:, None, None]
    caps_own = jnp.where(half_bits == 0, caps[0], turned)

    iterate = dot(leaf_inverse, rhs, ((1,), (0,)), HIGH)
    terms = dot(iterate, factors, ((0,), (1,)), HIGH)

    mine = lax.dynamic_slice_in_dim(terms, core * 256, 256, 0)
    theirs = lax.dynamic_slice_in_dim(terms, (1 - core) * 256, 256, 0)
    low = gram[448:576, :512]
    got = sent(
        jnp.concatenate([theirs, jnp.pad(low, ((0, 0), (0, RANK)))], axis=0), PARTNER[0]
    )
    low_got = got[256:, :512]
    both0, state = step(mine, got[:256], low[64:], low_got[64:], caps_own[0])
    gram1 = low[:64, :448] + low_got[:64, :448]

    part = y_low ^ y_high
    mine = lax.dynamic_slice_in_dim(state, part * 128, 128, 0)
    theirs = lax.dynamic_slice_in_dim(state, (1 - part) * 128, 128, 0)
    got = sent(jnp.concatenate([theirs, jnp.pad(gram1, ((0, 0), (0, RANK)))], axis=0), PARTNER[1])
    both1, state = step(mine, got[:128], gram1, got[128:, :448], caps_own[1])

    mine = lax.dynamic_slice_in_dim(state, y_high * 64, 64, 0)
    theirs = lax.dynamic_slice_in_dim(state, (1 - y_high) * 64, 64, 0)
    got = sent(theirs, PARTNER[2])
    lower2, upper2 = octet_sum[:64, :384], octet_sum[64:128, :384]
    own2 = jnp.where(y_high == 0, lower2, upper2)
    other2 = jnp.where(y_high == 0, upper2, lower2)
    both2, state = step(mine, got, own2, other2, caps_own[2])

    low_gathered = lax.all_gather(
        jnp.concatenate([both0, both1, both2], axis=0), "leaf", axis_index_groups=aligned(8, count)
    )

    gram3, gram4 = octet_sum[192:256, :320], octet_sum[128:192, :256]
    got = sent(jnp.concatenate([state, gram4, gram3], axis=1), PARTNER[3])
    both3, state = step(state, got[:, :384], gram3, got[:, 640:], caps_own[3])
    gram4 = gram4 + got[:, 384:640]

    got = sent(jnp.concatenate([gram4, state], axis=1), PARTNER[4])
    both4, state = step(state, got[:, 256:], gram4, got[:, :256], caps_own[4])

    got = sent(state, PARTNER[5])
    own5 = lax.dynamic_slice_in_dim(plane_sum, z_quarter * 64, 64, 0)[:, :192]
    other5 = lax.dynamic_slice_in_dim(plane_sum, (z_quarter ^ 1) * 64, 64, 0)[:, :192]
    both5, state = step(state, got, own5, other5, caps_own[5])

    got = sent(state, PARTNER[6])
    lower6, upper6 = plane_sum[256:, :128], plane_sum[256:, 128:]
    own6 = jnp.where(z_half == 0, lower6, upper6)
    other6 = jnp.where(z_half == 0, upper6, lower6)
    both6, state = step(state, got, own6, other6, caps_own[6])

    middle_gathered = lax.all_gather(
        jnp.concatenate([both6[:, :64], both5[:, :64], both4[:, :64], both3[:, :64]], axis=1),
        "leaf", axis_index_groups=aligned(8, count),
    )

    gram7 = plane_sum[:64, 192:]
    got = sent(jnp.concatenate([state, gram7], axis=1), PARTNER[7])
    both7, state = step(state, got[:, :128], gram7, got[:, 128:], caps_own[7])

    got = sent(state, PARTNER[8])
    both8, _ = step(state, got, None, None, caps_own[8])

    high_gathered = lax.all_gather(
        jnp.concatenate([both8[:, :64], both7[:, :64]], axis=1),
        "leaf", axis_index_groups=aligned(8, count),
    )

    def place(shard):
        c, b1, b2 = shard >> 2, shard >> 1 & 1, shard & 1
        return b2 << 2 | (b1 ^ b2) << 1 | c

    in_order = [place(s) for s in range(8)]
    octet_place = position & 7
    mine0 = both0[:, :64]
    partner0 = lax.dynamic_index_in_dim(low_gathered, octet_place ^ 1, 0, False)[:256, 64:]
    corr0 = jnp.where(
        core == 0,
        jnp.concatenate([mine0, partner0], axis=0),
        jnp.concatenate([partner0, mine0], axis=0),
    )
    pieces = []
    for c in range(2):
        for b1 in range(2):
            low_bit = b1 ^ y_high
            block = lax.dynamic_index_in_dim(
                low_gathered, y_high << 2 | low_bit << 1 | c, 0, False
            )[256:384]
            pieces.append(jnp.where(low_bit == y_low, block[:, :64], block[:, 64:]))
    corr1 = jnp.concatenate(pieces, axis=0)
    pieces = []
    for s in range(8):
        block = low_gathered[in_order[s], 384:]
        pieces.append(jnp.where(y_high == (s & 1), block[:, :64], block[:, 64:]))
    corr2 = jnp.concatenate(pieces, axis=0)
    middle = jnp.concatenate([middle_gathered[q] for q in in_order], axis=0)
    first = jnp.concatenate([middle, corr2, corr1, corr0], axis=1)
    iterate = iterate - dot(factors[128:], first, ((0,), (1,)), HIGH)
    last = jnp.concatenate([high_gathered[q] for q in in_order], axis=0)
    return iterate - dot(factors[:128], last, ((0,), (1,)), HIGH)


def solution(mesh):
    return jax.shard_map(
        local,
        mesh=mesh,
        in_specs=(P("leaf", None), P("leaf", None), P("leaf", None), P("leaf", None, None, None)),
        out_specs=P("leaf", None),
        check_vma=False,
    )
```

time: 422 us -> 555 us (1.32)
  waiting for transfers between devices: 224 us -> 420 us
  starting transfers between devices: 154 us -> 32.8 us
  blocking collectives: 0 us -> 29.2 us
  local copies, waits for them, and re-layouts: 1.94 us -> 24.6 us
  matrix products: 39.2 us -> 16.8 us
  between operations: 0.79 us -> 15.9 us
  other arithmetic: 0.86 us -> 14.1 us
    psum x0 -> x2, waiting for transfers between devices: none -> 370 us  [the longest x1 326 us: local(): lax.psum(plane_part, 'leaf', axis_index_groups=aligned(128, count))]
    ppermute x45 -> x9, waiting for transfers between devices: 224 us -> 50.4 us  [sent(): return lax.ppermute(array, 'leaf', [(i, i ^ mask) for i in range(count)])]
    ppermute x45 -> x9, starting transfers between devices: 154 us -> 32.7 us  [sent(): return lax.ppermute(array, 'leaf', [(i, i ^ mask) for i in range(count)])]
    all_gather x0 -> x2, blocking collectives: none -> 29.2 us  [the longest x1 14.9 us: local(): lax.all_gather(jnp.concatenate([both8[:, :64], both7[:, :64]], axis=1), '...]
    dot_general x28 -> x22, matrix products: 39.2 us -> 16.8 us  [dot(): lax.dot_general(a, b, ((dims[0], dims[1]), ((), ())), precision=precision...]
    slice x1 -> x32, local copies, waits for them, and re-layouts: 0.7 us -> 13.9 us  [the longest x2 2.04 us: local(): both0, state = step(mine, got[:256], low[64:], low_got[64:], caps_own[0])]
    select_n x9, other arithmetic: 0.18 us -> 6.45 us  [the longest x1 1.72 us: local(): jnp.where(z_quarter == s, row5, 0.0)]
  transfers between devices with their start and end apart: 45 -> 12, of which waited for: 45 -> 8; matrix products, arithmetic and copies ran while one was open for 0% -> 5% of each run, Pallas kernels for 0% -> 0%
where the time goes in v1:
time: 555 us; the launch traced here: 554 us
  waiting for transfers between devices  420 us (76%)
  starting transfers between devices  32.8 us (6%)
  blocking collectives  29.2 us (5%)
  local copies, waits for them, and re-layouts  24.6 us (4%)
  matrix products  16.8 us (3%)
  between operations  15.9 us (3%)
  other arithmetic  14.1 us (3%)
    psum x1, waiting for transfers between devices, local(): lax.psum(plane_part, 'leaf', axis_index_groups=aligned(128, count))  326 us
    ppermute x9, waiting for transfers between devices, sent(): return lax.ppermute(array, 'leaf', [(i, i ^ mask) for i in range(count)])  50.4 us
    psum x1, waiting for transfers between devices, local(): lax.psum(octet_part, 'leaf', axis_index_groups=aligned(8, count))  43.7 us
    ppermute x9, starting transfers between devices, sent(): return lax.ppermute(array, 'leaf', [(i, i ^ mask) for i in range(count)])  32.7 us
    dot_general x22, matrix products, dot(): lax.dot_general(a, b, ((dims[0], dims[1]), ((), ())), precision=precision...  16.8 us
    all_gather x1, blocking collectives, local(): lax.all_gather(jnp.concatenate([both8[:, :64], both7[:, :64]], axis=1), '...  14.9 us
    all_gather x1, blocking collectives, local(): lax.all_gather(jnp.concatenate([both6[:, :64], both5[:, :64], both4[:, :6...  14.3 us
  transfers between devices with their start and end apart: 12, of which 8 were waited for; matrix products, arithmetic and copies ran while one was open for 5% of the time, Pallas kernels for 0%

profile of v1, /device:TPU:1, one launch (start us, length us, event | category | flops | bytes accessed | tf_op | source)
XLA Modules:
  0.0 553.6 jit_solution(11676344239609946334)
XLA Ops:
  7.4 1.1 slice_dynamic-update-slice_fusion.13
  8.4 0.9 slice_dynamic-update-slice_fusion.11
  9.4 0.9 slice_dynamic-update-slice_fusion.9
  10.3 0.9 slice_dynamic-update-slice_fusion.7
  11.2 0.9 slice_dynamic-update-slice_fusion.5
  12.2 0.8 slice_dynamic-update-slice_fusion.1
  13.1 0.8 copy-done.5
  13.8 2.7 fusion.138
  16.6 1.0 fusion.136
  17.6 1.1 fusion.137
  18.7 1.6 slice.622
  20.4 1.0 select_maximum_fusion
  21.3 8.8 %collective-permute-start = (f32[384,576]{0,1:T(8,128)}, f32[384,576]{0,1:T(8,128)}, u32[]{:S(2)}, u32[]{:S(2)}) collective-permute-start(f32[384,576]{0,1:T(8,128)} %select_maximum_fusion), channel_id=1, source_target_pairs={{0,1},{1,0},{2,3},{3,2},{4,5},{5,4},{6,7},{7,6},{8,9},{9,8},{10,11... | collective-permute-start | bytes 2654216 | tf_op jit(solution)/shard_map/ppermute | solution.py:25
  30.1 0.9 slice.642
  31.1 1.0 slice_select_fusion.3
  32.0 0.9 pad_maximum_fusion.2
  33.1 1.0 slice.630
  34.1 1.4 slice.666
  35.6 1.2 fusion.134
  37.3 1.0 slice.624
  38.6 1.1 slice.631
  39.7 1.7 fusion.16
  41.4 1.2 slice_add_fusion.2
  42.7 1.9 collective-permute-start.1
  44.6 1.5 slice_select_fusion.15
  46.1 1.7 slice_select_fusion.7
  47.8 11.4 %collective-permute-done.1 = f32[192,512]{0,1:T(8,128)S(1)} collective-permute-done((f32[192,512]{0,1:T(8,128)S(1)}, f32[192,512]{0,1:T(8,128)S(1)}, u32[]{:S(2)}, u32[]{:S(2)}) %collective-permute-start.1) | collective-permute-done | bytes 393248 | tf_op jit(solution)/shard_map/ppermute | solution.py:25
  60.0 0.8 constant_dynamic-slice_fusion.2
  60.8 1.9 collective-permute-start.2
  62.7 43.7 %all-reduce.6.cloned.1.call-done = f32[256,384]{0,1:T(8,128)} async-done(((f32[256,384]{0,1:T(8,128)}), f32[256,384]{0,1:T(8,128)}) %all-reduce.6.cloned.1.call-update) | async-done | bytes 393232 | tf_op jit(solution)/shard_map/psum | solution.py:62
  106.4 1.1 slice_select_fusion.1
  107.5 1.0 slice.647
  108.6 0.9 slice.646
  109.6 0.7 copy-done.23
  110.6 1.3 fusion.36
  111.9 0.8 pad_maximum_fusion.1
  112.8 2.6 collective-permute-start.3
  115.5 0.9 fusion.17
  116.5 0.6 slice_bitcast_fusion
  117.1 326.1 %all-reduce.8.cloned.1.call-done = f32[320,256]{0,1:T(8,128)} async-done(((f32[320,256]{0,1:T(8,128)}), f32[320,256]{0,1:T(8,128)}) %all-reduce.8.cloned.1.call-update) | async-done | bytes 327696 | tf_op jit(solution)/shard_map/psum | solution.py:68
  443.3 0.8 slice.722
  444.0 0.8 slice.650
  445.1 1.0 slice_add_fusion.6
  446.1 0.9 slice.652
  447.1 1.3 fusion.43
  448.4 1.9 collective-permute-start.4
  450.3 0.7 slice_select_fusion.13
  451.0 14.4 %collective-permute-done.4 = f32[64,576]{0,1:T(8,128)S(1)} collective-permute-done((f32[64,576]{0,1:T(8,128)S(1)}, f32[64,576]{0,1:T(8,128)S(1)}, u32[]{:S(2)}, u32[]{:S(2)}) %collective-permute-start.4) | collective-permute-done | bytes 147488 | tf_op jit(solution)/shard_map/ppermute | solution.py:25
  466.0 3.5 collective-permute-start.5
  469.6 15.0 %collective-permute-done.5 = f32[64,256]{0,1:T(8,128)S(1)} collective-permute-done((f32[64,256]{0,1:T(8,128)S(1)}, f32[64,256]{0,1:T(8,128)S(1)}, u32[]{:S(2)}, u32[]{:S(2)}) %collective-permute-start.5) | collective-permute-done | bytes 65568 | tf_op jit(solution)/shard_map/ppermute | solution.py:25
  485.2 4.6 collective-permute-start.6
  489.8 0.7 pad_maximum_fusion.4
  490.6 5.1 collective-permute-done.6
  496.0 14.3 %all-gather = f32[512,256]{1,0:T(8,128)S(1)} all-gather(f32[64,256]{1,0:T(8,128)S(1)} %pad_maximum_fusion.6), channel_id=2, replica_groups={{0,1,2,3,4,5,6,7},{8,9,10,11,12,13,14,15},{16,17,18,19,20,21,22,23},{24..., dimensions={0}, use_global_device_ids=true | all-gather | bytes 589824 | tf_op jit(solution)/shard_map/all_gather | solution.py:124
  510.7 3.1 collective-permute-start.7
  513.8 3.1 collective-permute-done.7
  517.4 4.4 collective-permute-start.8
  521.8 1.5 collective-permute-done.8
  523.7 14.9 %all-gather.2 = f32[512,128]{1,0:T(8,128)S(1)} all-gather(f32[64,128]{1,0:T(8,128)S(1)} %pad_maximum_fusion.7), channel_id=4, replica_groups={{0,1,2,3,4,5,6,7},{8,9,10,11,12,13,14,15},{16,17,18,19,20,21,22,23},{24..., dimensions={0}, use_global_device_ids=true | all-gather | bytes 294912 | tf_op jit(solution)/shard_map/all_gather | solution.py:136
  538.7 0.6 fusion.25
  539.3 0.9 slice_bitcast_fusion.17
  540.3 1.0 dynamic-slice_bitcast_fusion
  541.9 1.0 dynamic-slice_bitcast_fusion.4
  543.2 3.0 fusion
  (140 shorter events, 6.6 us)
Async XLA Ops:
  7.4 9.2 %copy-start = (f32[512,512]{1,0:T(8,128)S(1)}, f32[512,512]{1,0:T(8,128)}, u32[]{:S(2)}) copy-start(f32[512,512]{1,0:T(8,128)} %param.5) | copy-start | bytes 3145732
  7.4 4.8 copy-start.3
  7.4 99.0 %all-reduce.6.cloned.1.call-start = ((), (), s32[]{:S(2)}) async-start(), calls=%async_computation | async-start | bytes 786432 | tf_op jit(solution)/shard_map/psum | solution.py:62
  12.9 0.9 copy-start.5
  13.8 2.7 copy-start.7
  18.7 16.8 %copy-start.1 = (f32[512,576]{0,1:T(8,128)}, f32[512,576]{0,1:T(8,128)S(1)}, u32[]{:S(2)}) copy-start(f32[512,576]{0,1:T(8,128)S(1)} %fusion.137) | copy-start | bytes 3538948
  21.3 15.9 %collective-permute-start = (f32[384,576]{0,1:T(8,128)}, f32[384,576]{0,1:T(8,128)}, u32[]{:S(2)}, u32[]{:S(2)}) collective-permute-start(f32[384,576]{0,1:T(8,128)} %select_maximum_fusion), channel_id=1, source_target_pairs={{0,1},{1,0},{2,3},{3,2},{4,5},{5,4},{6,7},{7,6},{8,9},{9,8},{10,11... | collective-permute-start | bytes 2654216 | tf_op jit(solution)/shard_map/ppermute | solution.py:25
  33.0 410.3 %all-reduce.8.cloned.1.call-start = ((), (), s32[]{:S(2)}) async-start(), calls=%async_computation.1 | async-start | bytes 786432 | tf_op jit(solution)/shard_map/psum | solution.py:68
  35.6 1.4 copy-start.4
  37.0 1.2 dynamic-slice-start
  37.0 2.7 copy-start.2
  42.7 16.6 %collective-permute-start.1 = (f32[192,512]{0,1:T(8,128)S(1)}, f32[192,512]{0,1:T(8,128)S(1)}, u32[]{:S(2)}, u32[]{:S(2)}) collective-permute-start(f32[192,512]{0,1:T(8,128)S(1)} %select_maximum_fusion.1), channel_id=1, source_target_pairs={{0,2},{1,3},{2,0},{3,1},{4,6},{5,7},{6,4},{7,5},{8,10},{9,11},{10,... | collective-permute-start | bytes 1179656 | tf_op jit(solution)/shard_map/ppermute | solution.py:25
  60.8 48.8 %collective-permute-start.2 = (f32[64,448]{0,1:T(8,128)}, f32[64,448]{0,1:T(8,128)S(1)}, u32[]{:S(2)}, u32[]{:S(2)}) collective-permute-start(f32[64,448]{0,1:T(8,128)} %constant_dynamic-slice_fusion.2), channel_id=1, source_target_pairs={{0,6},{1,7},{2,4},{3,5},{4,2},{5,3},{6,0},{7,1},{8,14},{9,15},{10,... | collective-permute-start | bytes 344072 | tf_op jit(solution)/shard_map/ppermute | solution.py:25
  109.5 5.9 %copy-start.12 = (f32[64,192]{0,1:T(8,128)S(1)}, f32[64,192]{0,1:T(8,128)}, u32[]{:S(2)}) copy-start(f32[64,192]{0,1:T(8,128)} %get-tuple-element.19) | copy-start | bytes 147460
  109.5 5.9 %copy-start.13 = (f32[64,192]{0,1:T(8,128)S(1)}, f32[64,192]{0,1:T(8,128)}, u32[]{:S(2)}) copy-start(f32[64,192]{0,1:T(8,128)} %get-tuple-element.20) | copy-start | bytes 147460
  109.5 5.9 %copy-start.14 = (f32[64,192]{0,1:T(8,128)S(1)}, f32[64,192]{0,1:T(8,128)}, u32[]{:S(2)}) copy-start(f32[64,192]{0,1:T(8,128)} %get-tuple-element.21) | copy-start | bytes 147460
  109.5 5.9 %copy-start.15 = (f32[64,192]{0,1:T(8,128)S(1)}, f32[64,192]{0,1:T(8,128)}, u32[]{:S(2)}) copy-start(f32[64,192]{0,1:T(8,128)} %get-tuple-element.22) | copy-start | bytes 147460
  109.5 5.9 %copy-start.21 = (f32[64,128]{0,1:T(8,128)S(1)}, f32[64,128]{0,1:T(8,128)}, u32[]{:S(2)}) copy-start(f32[64,128]{0,1:T(8,128)} %get-tuple-element.23) | copy-start | bytes 98308
  109.5 5.9 %copy-start.22 = (f32[64,128]{0,1:T(8,128)S(1)}, f32[64,128]{0,1:T(8,128)}, u32[]{:S(2)}) copy-start(f32[64,128]{0,1:T(8,128)} %get-tuple-element.24) | copy-start | bytes 98308
  109.5 5.9 %copy-start.25 = (f32[64,64]{0,1:T(8,128)S(1)}, f32[64,64]{0,1:T(8,128)}, u32[]{:S(2)}) copy-start(f32[64,64]{0,1:T(8,128)} %slice.666) | copy-start | bytes 49156
  109.6 0.7 copy-start.23
  112.8 331.3 %collective-permute-start.3 = (f32[64,960]{0,1:T(8,128)}, f32[64,960]{0,1:T(8,128)}, u32[]{:S(2)}, u32[]{:S(2)}) collective-permute-start(f32[64,960]{0,1:T(8,128)} %pad_maximum_fusion.1), channel_id=1, source_target_pairs={{0,8},{1,9},{2,10},{3,11},{4,12},{5,13},{6,14},{7,15},{8,0},{9,1},... | collective-permute-start | bytes 737288 | tf_op jit(solution)/shard_map/ppermute | solution.py:25
  116.4 422.9 %all-gather.5.cloned.1.call-start = ((), (), s32[]{:S(2)}) async-start(), calls=%async_computation.2 | async-start | bytes 2064384 | tf_op jit(solution)/shard_map/all_gather | solution.py:101
  444.0 6.3 %copy-start.16 = (f32[320,256]{0,1:T(8,128)S(1)}, f32[320,256]{0,1:T(8,128)}, u32[]{:S(2)}) copy-start(f32[320,256]{0,1:T(8,128)} %all-reduce.8.cloned.1.call-done) | copy-start | bytes 983044
  445.1 5.8 %copy-start.17 = (f32[64,128]{1,0:T(8,128)}, f32[64,128]{1,0:T(8,128)S(1)}, u32[]{:S(2)}) copy-start(f32[64,128]{1,0:T(8,128)S(1)} %fusion.73) | copy-start | bytes 98308
  448.4 17.0 %collective-permute-start.4 = (f32[64,576]{0,1:T(8,128)S(1)}, f32[64,576]{0,1:T(8,128)S(1)}, u32[]{:S(2)}, u32[]{:S(2)}) collective-permute-start(f32[64,576]{0,1:T(8,128)S(1)} %pad_maximum_fusion.3), channel_id=1, source_target_pairs={{0,16},{1,17},{2,18},{3,19},{4,20},{5,21},{6,22},{7,23},{8,24},{9,... | collective-permute-start | bytes 442376 | tf_op jit(solution)/shard_map/ppermute | solution.py:25
  465.9 30.0 %copy-start.18 = (f32[64,128]{1,0:T(8,128)S(1)}, f32[64,128]{1,0:T(8,128)}, u32[]{:S(2)}) copy-start(f32[64,128]{1,0:T(8,128)} %copy-done.17) | copy-start | bytes 98308
  466.0 18.6 %collective-permute-start.5 = (f32[64,256]{0,1:T(8,128)S(1)}, f32[64,256]{0,1:T(8,128)S(1)}, u32[]{:S(2)}, u32[]{:S(2)}) collective-permute-start(f32[64,256]{0,1:T(8,128)S(1)} %fusion.50), channel_id=1, source_target_pairs={{0,32},{1,33},{2,34},{3,35},{4,36},{5,37},{6,38},{7,39},{8,40},{9,... | collective-permute-start | bytes 196616 | tf_op jit(solution)/shard_map/ppermute | solution.py:25
  485.2 25.2 %copy-start.19 = (f32[64,128]{0,1:T(8,128)S(1)}, f32[64,128]{0,1:T(8,128)}, u32[]{:S(2)}) copy-start(f32[64,128]{0,1:T(8,128)} %get-tuple-element.31) | copy-start | bytes 98308
  485.2 25.2 %copy-start.20 = (f32[64,128]{0,1:T(8,128)S(1)}, f32[64,128]{0,1:T(8,128)}, u32[]{:S(2)}) copy-start(f32[64,128]{0,1:T(8,128)} %get-tuple-element.32) | copy-start | bytes 98308
  485.2 10.4 %collective-permute-start.6 = (f32[64,192]{0,1:T(8,128)S(1)}, f32[64,192]{0,1:T(8,128)S(1)}, u32[]{:S(2)}, u32[]{:S(2)}) collective-permute-start(f32[64,192]{0,1:T(8,128)S(1)} %fusion.61), channel_id=1, source_target_pairs={{0,96},{1,97},{2,98},{3,99},{4,100},{5,101},{6,102},{7,103},{8,104... | collective-permute-start | bytes 147464 | tf_op jit(solution)/shard_map/ppermute | solution.py:25
  510.3 13.0 %copy-start.24 = (f32[128,128]{1,0:T(8,128)S(1)}, f32[128,128]{1,0:T(8,128)}, u32[]{:S(2)}) copy-start(f32[128,128]{1,0:T(8,128)} %slice_bitcast_fusion) | copy-start | bytes 196612
  510.4 28.3 %copy-start.10 = (f32[64,512]{1,0:T(8,128)S(1)}, f32[64,512]{1,0:T(8,128)}, u32[]{:S(2)}) copy-start(f32[64,512]{1,0:T(8,128)} %get-tuple-element.27) | copy-start | bytes 393220
  510.4 28.3 %copy-start.11 = (f32[64,512]{1,0:T(8,128)S(1)}, f32[64,512]{1,0:T(8,128)}, u32[]{:S(2)}) copy-start(f32[64,512]{1,0:T(8,128)} %get-tuple-element.28) | copy-start | bytes 393220
  510.7 6.2 %collective-permute-start.7 = (f32[64,192]{0,1:T(8,128)S(1)}, f32[64,192]{0,1:T(8,128)S(1)}, u32[]{:S(2)}, u32[]{:S(2)}) collective-permute-start(f32[64,192]{0,1:T(8,128)S(1)} %pad_maximum_fusion.5), channel_id=1, source_target_pairs={{0,128},{1,129},{2,130},{3,131},{4,132},{5,133},{6,134},{7,135},{8... | collective-permute-start | bytes 147464 | tf_op jit(solution)/shard_map/ppermute | solution.py:25
  517.4 5.9 %collective-permute-start.8 = (f32[64,64]{0,1:T(8,128)S(1)}, f32[64,64]{0,1:T(8,128)S(1)}, u32[]{:S(2)}, u32[]{:S(2)}) collective-permute-start(f32[64,64]{0,1:T(8,128)S(1)} %fusion.108), channel_id=1, source_target_pairs={{0,384},{1,385},{2,386},{3,387},{4,388},{5,389},{6,390},{7,391},{8... | collective-permute-start | bytes 49160 | tf_op jit(solution)/shard_map/ppermute | solution.py:25
  521.8 16.8 %copy-start.8 = (f32[512,256]{1,0:T(8,128)}, f32[512,256]{1,0:T(8,128)S(1)}, u32[]{:S(2)}) copy-start(f32[512,256]{1,0:T(8,128)S(1)} %constant_dynamic-update-slice_fusion.2) | copy-start | bytes 1572868
  541.5 1.7 copy-start.6
  541.5 1.7 copy-start.9
Sparse Core Ops, SparseCore 0:
  33.1 73.2 all-reduce.5
  490.7 29.2 all-gather.4
Sparse Core Ops, SparseCore 1:
  116.5 326.7 all-reduce.7
